TPU v7x, 128 devices: a whole 4x4x4 slice. The times are simulated.
128 devices in a mesh: branch: 128 (over x, y, z, core).
Axes of the slice: x: 4, y: 4, z: 4, core: 2. Of those that a mesh axis runs over, the one named last changes fastest.
Arguments:
- points: float32 [3, 4194304], P(None, 'branch'), may hold values from 0 to 1
- charges: float32 [8, 4194304], P(None, 'branch'), may hold values from -6 to 6
- leaf_basis: bfloat16 [32768, 32, 128], P('branch'), may hold values from -0.5 to 0.5
- low_transfer: bfloat16 [65280, 1024], P('branch'), may hold values from -1 to 1
- low_coupling: bfloat16 [65408, 8, 1024], P('branch'), may hold values from -0.375 to 0.375
- low_partner: int32 [65408, 8], P('branch'), may hold values from -1 to 65407, as said below
- top_transfer: bfloat16 [252, 1024], replicated, may hold values from -1 to 1
- top_coupling: bfloat16 [126, 4, 1024], replicated, may hold values from -0.53033009 to 0.53033009
- top_partner: int32 [126, 4], replicated, may hold values from -1 to 63, as said below
- near_list: int32 [32768, 8], P('branch'), may hold values from -1 to 32767, as said below
Outputs:
- potential: float32 [8, 4194304], P(None, 'branch')
Inputs may be any that keep to these rules, and one draw needn't show every extreme that they name: `low_partner`: row b * 511 + position lists coupling partners of that node of block b: each entry is -1 or the global id of another node of the same level k; numbering the nodes of level k of all blocks end to end (block by block), the partner's number differs from the node's own by 1 to max(1, 64 / 2^k) (integer division). The first entry is never -1. `top_partner`: each entry is -1 or the index, within its level, of another node of the same level; the first entry is never -1. `near_list`: entry 0 of leaf g's list is g; every other entry is -1 or a leaf within 64 leaves of g.
All inputs are finite; a program needn't handle non-finite values.
Results may differ from a plain program's by a relative error of at most 0.004.
Values sent between devices are 32-bit elements; how exact they have to be, the bound alone decides.
A program may use at most 256 MiB of HBM per device.

v0:
```python
import math

import jax
import jax.numpy as jnp
from jax import lax
from jax.experimental import pallas as pl
from jax.experimental.pallas import tpu as pltpu
from jax.sharding import PartitionSpec as P

SOFTEN = 0.0025
FOURPI = 4.0 * math.pi
F32 = jnp.float32
BF16 = jnp.bfloat16
VMEM_BYTES = 60 << 20
GROUP = 32


def level_start(total, depth_at):
    return 2 * total - (2 * total >> depth_at)


def halo_counts(leaves, depth):
    return [max(1, (leaves // 4) >> k) for k in range(depth + 1)]


def lane_group(shape):
    return lax.broadcasted_iota(jnp.int32, shape, len(shape) - 1) // 32


def spread_groups(z):
    z = z + pltpu.roll(z, 32, axis=z.ndim - 1)
    return z + pltpu.roll(z, 64, axis=z.ndim - 1)


def expand_matrix():
    r = lax.broadcasted_iota(jnp.int32, (128, 1024), 0)
    c = lax.broadcasted_iota(jnp.int32, (128, 1024), 1)
    return jnp.where(((r % 32) == (c // 32)) & (r < 96), 1.0, 0.0).astype(BF16)


def reduce_matrix():
    r = lax.broadcasted_iota(jnp.int32, (1024, 128), 0)
    c = lax.broadcasted_iota(jnp.int32, (1024, 128), 1)
    return jnp.where((r // 32) == (c % 32), 1.0, 0.0).astype(BF16)


def expand(u, xmat):
    hi = u.astype(BF16).astype(F32)
    rest = u - hi
    mid = rest.astype(BF16).astype(F32)
    low = rest - mid
    group = lane_group(u.shape)
    parts = jnp.where(group == 0, hi, jnp.where(group == 1, mid, jnp.where(group == 2, low, 0.0)))
    return jnp.dot(parts.astype(BF16), xmat, preferred_element_type=F32)


def reduce32(acc, rmat):
    hi = acc.astype(BF16)
    low = (acc - hi.astype(F32)).astype(BF16)
    return jnp.dot(hi, rmat, preferred_element_type=F32) + jnp.dot(
        low, rmat, preferred_element_type=F32
    )


def point_rows(points):
    n = points.shape[1]
    row = lax.broadcasted_iota(jnp.int32, (8, n), 0)
    scaled = (points - 0.5) * FOURPI
    value = jnp.where(
        row == 0, scaled[0:1], jnp.where(row == 1, scaled[1:2], jnp.where(row == 2, scaled[2:3], 0.0))
    )
    high = value.astype(BF16).astype(F32)
    low = (value - high).astype(BF16).astype(F32)
    both = high + low
    norm = jnp.sum(both * both, axis=0, keepdims=True)
    return row, high, low, norm


def three_parts(norm):
    one = norm.astype(BF16).astype(F32)
    rest = norm - one
    two = rest.astype(BF16).astype(F32)
    return one, two, rest - two


def source_rows(row, high, low, norm):
    m1, m2, m3 = three_parts(norm)
    unit = row == 4
    s0 = jnp.where(row == 3, m1, jnp.where(unit, 1.0, high))
    s1 = jnp.where(row == 3, m2, jnp.where(unit, 1.0, low))
    s2 = jnp.where(row == 3, m3, jnp.where(unit, 1.0, high))
    return jnp.concatenate([s0, s1, s2, low], axis=0).astype(BF16)


def target_rows(row, high, low, norm):
    n1, n2, n3 = three_parts(norm + SOFTEN * FOURPI * FOURPI)
    unit = row == 3
    t0 = jnp.where(row == 4, n1, jnp.where(unit, 1.0, -2.0 * high))
    t1 = jnp.where(row == 4, n2, jnp.where(unit, 1.0, -2.0 * high))
    t2 = jnp.where(row == 4, n3, jnp.where(unit, 1.0, -2.0 * low))
    return jnp.concatenate([t0, t1, t2, -2.0 * low], axis=0).astype(BF16)


def spread_row(ref, at):
    return ref[pl.ds(at, 8, stride=0), :]


def move_up(u_ref, e_ref, xmat_ref, src, dst, e_row, width):
    group = min(GROUP, width)

    def step(i, carry):
        first = i * group
        mats = e_ref.at[pl.ds(pl.multiple_of(e_row + first, 8), group)] if group >= 8 else e_ref
        skip = 0 if group >= 8 else e_row
        u = u_ref[pl.ds(src + first, group)].reshape(group * 8, 128)
        wide = expand(u, xmat_ref[...])
        for n in range(0, group, 2):
            total = None
            for m in (n, n + 1):
                prod = wide[8 * m : 8 * m + 8] * spread_row(mats, skip + m)
                for j in range(8):
                    piece = prod[:, 128 * j : 128 * j + 128]
                    total = piece if total is None else total + piece
            u_ref[dst + i * (group // 2) + n // 2] = spread_groups(total)
        return carry

    if width == group:
        step(0, 0)
    else:
        lax.fori_loop(0, width // group, step, 0)


def upcast_rows(dst_ref, src_ref, rows):
    for first in range(0, rows, 64):
        count = min(64, rows - first)
        dst_ref[first : first + count, :] = src_ref[first : first + count, :].astype(F32)


def rounds_of(branches):
    rounds, stride = [], 1
    while stride < branches:
        size = 2 if stride == 1 or branches // stride == 2 else 4
        rounds.append((size, stride))
        stride *= size
    return rounds


def make_product(leaves, branches, near_slots, slots, top_slots):
    depth = leaves.bit_length() - 1
    depth_top = branches.bit_length() - 1
    counts = halo_counts(leaves, depth)
    packs = -(-sum(counts) // 4)
    rows = 2 * leaves - 1
    own = rows
    reach = leaves // 4
    span = leaves + 2 * reach
    edge = reach * 128
    length = leaves * 128
    unroll = 4
    wide = near_slots * 128
    top_rows = 2 * branches - 4
    rounds = rounds_of(branches)
    n_round = sum(size - 1 for size, _ in rounds)
    loop_steps = leaves // (2 * unroll)

    def kernel(
        index_ref,
        partner_ref,
        top_partner_ref,
        pts_ref,
        chg_ref,
        basis_hbm,
        transfer_hbm,
        coupling_hbm,
        top_transfer_hbm,
        top_coupling_hbm,
        out_ref,
        basis_ref,
        transfer_ref,
        coupling_ref,
        top_transfer_ref,
        top_coupling_ref,
        pts_before_ref,
        pts_after_ref,
        chg_before_ref,
        chg_after_ref,
        last_ref,
        first_ref,
        before_ref,
        after_ref,
        table_ref,
        upper_ref,
        far_ref,
        e_ref,
        top_e_ref,
        src_ref,
        tgt_ref,
        load_ref,
        tile_ref,
        rhs_ref,
        c_ref,
        acc_ref,
        xmat_ref,
        rmat_ref,
        load_sem,
        send_sem,
        recv_sem,
    ):
        me = lax.axis_index("branch")
        fetches = [
            pltpu.make_async_copy(a, b, load_sem.at[i])
            for i, (a, b) in enumerate(
                (
                    (basis_hbm, basis_ref),
                    (transfer_hbm, transfer_ref),
                    (coupling_hbm, coupling_ref.at[0:rows]),
                    (top_transfer_hbm, top_transfer_ref),
                    (top_coupling_hbm, top_coupling_ref),
                )
            )
        ]
        for fetch in fetches:
            fetch.start()

        right = (me + 1) % branches
        left = (me + branches - 1) % branches
        peers = []
        for size, stride in rounds:
            digit = (me // stride) % size
            for t in range(1, size):
                peers.append(me + ((digit + t) % size - digit) * stride)
        barrier = pltpu.get_barrier_semaphore()
        for other in [left, right] + peers:
            pl.semaphore_signal(
                barrier, inc=1, device_id=(other,), device_id_type=pl.DeviceIdType.MESH
            )

        def remote(i, a, b, other):
            return pltpu.make_async_remote_copy(
                src_ref=a,
                dst_ref=b,
                send_sem=send_sem.at[i],
                recv_sem=recv_sem.at[i],
                device_id=(other,),
                device_id_type=pl.DeviceIdType.MESH,
            )

        halos = [
            remote(0, pts_ref.at[:, length - edge : length], pts_before_ref, right),
            remote(1, chg_ref.at[:, length - edge : length], chg_before_ref, right),
            remote(2, pts_ref.at[:, 0:edge], pts_after_ref, left),
            remote(3, chg_ref.at[:, 0:edge], chg_after_ref, left),
        ]
        coef_halos = [
            remote(4, last_ref, before_ref, right),
            remote(5, first_ref, after_ref, left),
        ]
        gathers, at = [], 0
        for size, stride in rounds:
            block = pl.ds((me // stride) * stride, stride)
            gathers.append(
                [
                    remote(6 + at + t, upper_ref.at[block], upper_ref.at[block], peers[at + t])
                    for t in range(size - 1)
                ]
            )
            at += size - 1

        xmat_ref[...] = expand_matrix()
        rmat_ref[...] = reduce_matrix()

        fetches[0].wait()

        def leaf_up(i, carry):
            at = pl.multiple_of(i * 1024, 1024)
            loads = chg_ref[:, pl.ds(at, 1024)]
            loads = jnp.concatenate([loads[:, 128 * g : 128 * g + 128] for g in range(8)], axis=0)
            basis = basis_ref[pl.ds(pl.multiple_of(i * 256, 256), 256), :]
            out = lax.dot_general(
                loads.astype(BF16), basis, (((1,), (1,)), ((), ())), preferred_element_type=F32
            )
            group = lane_group((8, 128))
            for g in range(8):
                piece = out[8 * g : 8 * g + 8, 128 * (g // 4) : 128 * (g // 4) + 128]
                table_ref[own + i * 8 + g] = spread_groups(jnp.where(group == g % 4, piece, 0.0))
            return carry

        lax.fori_loop(0, leaves // 8, leaf_up, 0, unroll=4)

        pl.semaphore_wait(barrier, 2 + len(peers))
        for copy in halos:
            copy.start()

        fetches[1].wait()
        upcast_rows(e_ref, transfer_ref, rows - 1)
        for k in range(depth):
            start = level_start(leaves, k)
            move_up(
                table_ref,
                e_ref,
                xmat_ref,
                own + start,
                own + level_start(leaves, k + 1),
                start,
                leaves >> k,
            )

        lane = lane_group((8, 128))
        for pack_ref, tail in ((last_ref, True), (first_ref, False)):
            nodes = []
            for k in range(depth + 1):
                start, width = level_start(leaves, k), leaves >> k
                begin = start + width - counts[k] if tail else start
                nodes += list(range(begin, begin + counts[k]))
            for at in range(0, len(nodes), 4):
                four = nodes[at : at + 4]
                packed = table_ref[own + four[0]]
                for g in range(1, len(four)):
                    packed = jnp.where(lane == g, table_ref[own + four[g]], packed)
                pack_ref[at // 4] = packed
        for copy in coef_halos:
            copy.start()
        upper_ref[pl.ds(me, 1)] = table_ref[own + rows - 1 : own + rows]
        for copy in gathers[0]:
            copy.start()

        def prepare(points, charges, first, is_own, count):
            def step(i, carry):
                at = pl.multiple_of(i * 1024, 1024)
                parts = point_rows(points[:, pl.ds(at, 1024)])
                source = source_rows(*parts)
                loads = charges[:, pl.ds(at, 1024)]
                for g in range(8):
                    src_ref[first + i * 8 + g] = source[:, 128 * g : 128 * g + 128]
                    load_ref[first + i * 8 + g] = loads[:, 128 * g : 128 * g + 128]
                if is_own:
                    target = target_rows(*parts)
                    for g in range(8):
                        tgt_ref[i * 8 + g] = target[:, 128 * g : 128 * g + 128]
                return carry

            lax.fori_loop(0, count // 8, step, 0)

        prepare(pts_ref, chg_ref, reach, True, leaves)
        for copy in halos:
            copy.wait_recv()
        prepare(pts_before_ref, chg_before_ref, 0, False, reach)
        prepare(pts_after_ref, chg_after_ref, reach + leaves, False, reach)
        src_ref[span] = src_ref[reach]
        load_ref[span] = jnp.zeros((8, 128), F32)

        def tiles_of(leaf, slot, j):
            target = tgt_ref[leaf]
            for s in range(near_slots):
                q = index_ref[leaf * near_slots + s]
                square = lax.dot_general(
                    src_ref[q], target, (((0,), (0,)), ((), ())), preferred_element_type=F32
                )
                tile_ref[slot, j, 128 * s : 128 * s + 128, :] = lax.rsqrt(square).astype(BF16)
                rhs_ref[slot, j, :, 128 * s : 128 * s + 128] = load_ref[q]

        def apply(leaf, slot, j):
            at = pl.multiple_of(leaf * 128, 128)
            out_ref[:, pl.ds(at, 128)] = jnp.dot(
                rhs_ref[slot, j].astype(BF16), tile_ref[slot, j], preferred_element_type=F32
            )

        for j in range(unroll):
            tiles_of(j, 0, j)

        def near_step(i, carry):
            for half in range(2):
                base = (2 * i + half) * unroll
                for j in range(unroll):
                    tiles_of((base + unroll + j) % leaves, 1 - half, j)
                for j in range(unroll):
                    apply(base + j, half, j)
            for r in range(1, len(rounds)):

                @pl.when(i == (r * loop_steps) // (len(rounds) + 1))
                def _():
                    for copy in gathers[r - 1]:
                        copy.wait_recv()
                    for copy in gathers[r]:
                        copy.start()

            return carry

        lax.fori_loop(0, loop_steps, near_step, 0)

        table_ref[3 * rows] = jnp.zeros((8, 128), F32)
        for copy in coef_halos:
            copy.wait_recv()
        for in_ref, tail, base in ((before_ref, True, 0), (after_ref, False, 2 * rows)):
            at = 0
            for k in range(depth + 1):
                start, width = level_start(leaves, k), leaves >> k
                begin = base + (start + width - counts[k] if tail else start)
                for i in range(counts[k]):
                    packed = in_ref[(at + i) // 4]
                    table_ref[begin + i] = spread_groups(
                        jnp.where(lane == (at + i) % 4, packed, 0.0)
                    )
                at += counts[k]

        coupling_ref[rows] = jnp.zeros((slots, 1024), BF16)
        fetches[2].wait()

        def couple(i, carry):
            first = i * 16
            c_ref[...] = coupling_ref[pl.ds(first, 16)].reshape(16 * slots, 1024).astype(F32)
            for n in range(16):
                acc = [None] * 8
                for s in range(slots):
                    u = table_ref[partner_ref[(first + n) * slots + s]]
                    row = spread_row(c_ref, n * slots + s)
                    for j in range(8):
                        piece = u * row[:, 128 * j : 128 * j + 128]
                        acc[j] = piece if acc[j] is None else acc[j] + piece
                for j in range(8):
                    acc_ref[8 * n : 8 * n + 8, 128 * j : 128 * j + 128] = acc[j]
            far = reduce32(acc_ref[0:128], rmat_ref[...])
            far_ref[pl.ds(first, 16)] = far.reshape(16, 8, 128)
            return carry

        lax.fori_loop(0, 2 * leaves // 16, couple, 0)

        fetches[3].wait()
        fetches[4].wait()
        upcast_rows(top_e_ref, top_transfer_ref, top_rows)
        for copy in gathers[-1]:
            copy.wait_recv()
        for u in range(depth_top - 1):
            src = level_start(branches, u)
            move_up(
                upper_ref, top_e_ref, xmat_ref, src, level_start(branches, u + 1), src, branches >> u
            )
        upper_ref[2 * branches - 2] = jnp.zeros((8, 128), F32)
        for u in range(1, depth_top):
            row_at = level_start(branches, u) - branches + me // (1 << u)
            mats = top_coupling_ref[row_at].astype(F32)
            acc = [None] * 8
            for s in range(top_slots):
                entry = top_partner_ref[row_at * top_slots + s]
                at = jnp.where(entry >= 0, level_start(branches, u) + entry, 2 * branches - 2)
                value = upper_ref[at]
                for j in range(8):
                    piece = value * mats[s : s + 1, 128 * j : 128 * j + 128]
                    acc[j] = piece if acc[j] is None else acc[j] + piece
            for j in range(8):
                acc_ref[8 * u - 8 : 8 * u, 128 * j : 128 * j + 128] = acc[j]
        far_top = reduce32(acc_ref[0 : 8 * (depth_top - 1)], rmat_ref[...])

        def down(value, row):
            return reduce32(jnp.concatenate([value] * 8, axis=1) * row, rmat_ref[...])

        current = far_top[8 * (depth_top - 2) :]
        for u in range(depth_top - 2, 0, -1):
            row = top_e_ref[pl.ds(level_start(branches, u) + me // (1 << u), 1), :]
            current = far_top[8 * u - 8 : 8 * u] + down(current, row)
        far_ref[rows - 1] = far_ref[rows - 1] + down(current, top_e_ref[pl.ds(me, 1), :])

        for k in range(depth - 1, -1, -1):
            start, width = level_start(leaves, k), leaves >> k
            parents = level_start(leaves, k + 1)
            size = min(GROUP, width)

            def level(i, carry, start=start, parents=parents, size=size):
                at = pl.multiple_of(start + i * size, 8) if size >= 8 else 0
                mats = e_ref.at[pl.ds(at, size)] if size >= 8 else e_ref
                skip = 0 if size >= 8 else start
                for n in range(size):
                    value = far_ref[parents + i * (size // 2) + n // 2]
                    row = spread_row(mats, skip + n)
                    for j in range(8):
                        acc_ref[8 * n : 8 * n + 8, 128 * j : 128 * j + 128] = (
                            value * row[:, 128 * j : 128 * j + 128]
                        )
                moved = reduce32(acc_ref[0 : 8 * size], rmat_ref[...])
                at = pl.ds(start + i * size, size)
                far_ref[at] = far_ref[at] + moved.reshape(size, 8, 128)
                return carry

            if width == size:
                level(0, 0)
            else:
                lax.fori_loop(0, width // size, level, 0)

        def leaf_down(i, carry):
            pieces = []
            for g in range(8):
                only = jnp.where(lane == g % 4, far_ref[i * 8 + g], 0.0)
                none = jnp.zeros((8, 128), F32)
                pieces.append(jnp.concatenate([only, none] if g < 4 else [none, only], axis=1))
            coefs = jnp.concatenate(pieces, axis=0).astype(BF16)
            basis = basis_ref[pl.ds(pl.multiple_of(i * 256, 256), 256), :]
            values = jnp.dot(coefs, basis, preferred_element_type=F32)
            for g in range(8):
                at = pl.ds(pl.multiple_of((i * 8 + g) * 128, 128), 128)
                out_ref[:, at] = out_ref[:, at] + values[8 * g : 8 * g + 8]
            return carry

        lax.fori_loop(0, leaves // 8, leaf_down, 0, unroll=4)
        for copy in halos + coef_halos + [copy for group in gathers for copy in group]:
            copy.wait_send()

    smem = pl.BlockSpec(memory_space=pltpu.SMEM)
    vmem = pl.BlockSpec(memory_space=pltpu.VMEM)
    hbm = pl.BlockSpec(memory_space=pl.ANY)
    n_copies = 6 + n_round
    return pl.pallas_call(
        kernel,
        out_shape=jax.ShapeDtypeStruct((8, length), F32),
        in_specs=[smem] * 3 + [vmem] * 2 + [hbm] * 5,
        out_specs=vmem,
        scratch_shapes=[
            pltpu.VMEM((leaves * 32, 128), BF16),
            pltpu.VMEM((rows - 1, 1024), BF16),
            pltpu.VMEM((rows + 1, slots, 1024), BF16),
            pltpu.VMEM((top_rows, 1024), BF16),
            pltpu.VMEM((branches - 2, top_slots, 1024), BF16),
            pltpu.VMEM((3, edge), F32),
            pltpu.VMEM((3, edge), F32),
            pltpu.VMEM((8, edge), F32),
            pltpu.VMEM((8, edge), F32),
            pltpu.VMEM((packs, 8, 128), F32),
            pltpu.VMEM((packs, 8, 128), F32),
            pltpu.VMEM((packs, 8, 128), F32),
            pltpu.VMEM((packs, 8, 128), F32),
            pltpu.VMEM((3 * rows + 1, 8, 128), F32),
            pltpu.VMEM((2 * branches - 1, 8, 128), F32),
            pltpu.VMEM((rows + 1, 8, 128), F32),
            pltpu.VMEM((rows - 1, 1024), F32),
            pltpu.VMEM((top_rows, 1024), F32),
            pltpu.VMEM((span + 1, 32, 128), BF16),
            pltpu.VMEM((leaves, 32, 128), BF16),
            pltpu.VMEM((span + 1, 8, 128), F32),
            pltpu.VMEM((2, unroll, wide, 128), BF16),
            pltpu.VMEM((2, unroll, 8, wide), F32),
            pltpu.VMEM((16 * slots, 1024), F32),
            pltpu.VMEM((8 * GROUP, 1024), F32),
            pltpu.VMEM((128, 1024), BF16),
            pltpu.VMEM((1024, 128), BF16),
            pltpu.SemaphoreType.DMA((5,)),
            pltpu.SemaphoreType.DMA((n_copies,)),
            pltpu.SemaphoreType.DMA((n_copies,)),
        ],
        compiler_params=pltpu.CompilerParams(
            vmem_limit_bytes=VMEM_BYTES, collective_id=0, has_side_effects=True
        ),
        cost_estimate=pl.CostEstimate(
            flops=4 * 10**10,
            bytes_accessed=16 << 20,
            transcendentals=leaves * near_slots * 128 * 128,
        ),
        name="product",
    )


def on_device(
    points,
    charges,
    leaf_basis,
    low_transfer,
    low_coupling,
    low_partner,
    top_transfer,
    top_coupling,
    top_partner,
    near_list,
):
    branches = lax.axis_size("branch")
    me = lax.axis_index("branch")
    leaves = leaf_basis.shape[0]
    rows = 2 * leaves - 1
    reach = leaves // 4
    near_rows = jnp.where(near_list >= 0, near_list - (me * leaves - reach), leaves + 2 * reach)
    partner_rows = jnp.where(low_partner >= 0, low_partner - (me - 1) * rows, 3 * rows)
    partner_rows = jnp.pad(partner_rows, ((0, 1), (0, 0)), constant_values=3 * rows)
    return make_product(
        leaves, branches, near_list.shape[1], low_partner.shape[1], top_partner.shape[1]
    )(
        near_rows.reshape(-1),
        partner_rows.reshape(-1),
        top_partner.reshape(-1),
        points,
        charges,
        leaf_basis.reshape(leaves * 32, 128),
        low_transfer,
        low_coupling,
        top_transfer,
        top_coupling,
    )


def solution(mesh):
    return jax.shard_map(
        on_device,
        mesh=mesh,
        in_specs=(
            P(None, "branch"),
            P(None, "branch"),
            P("branch", None, None),
            P("branch", None),
            P("branch", None, None),
            P("branch", None),
            P(),
            P(),
            P(),
            P("branch", None),
        ),
        out_specs=P(None, "branch"),
        check_vma=False,
    )
```

profile of v0, /device:TPU:0, one launch (start us, length us, event | category | flops | bytes accessed | tf_op | source)
XLA Modules:
  0.0 101.3 jit_solution(12524445564294908803)
XLA Ops:
  0.0 0.7 subtract_select_fusion.1
  0.7 0.7 subtract_select_fusion
  1.4 0.8 copy.13
  2.2 0.7 reshape.14.top_partner_ref
  2.9 0.1 copy.11
  3.0 0.7 reshape.12.index_ref
  3.8 0.1 copy.14
  3.9 0.8 reshape.13.partner_ref
  4.7 94.3 %product.1 = f32[8,32768]{1,0:T(8,128)} custom-call(s32[2048]{0:T(1024)} %reshape.12.index_ref, s32[4096]{0:T(1024)} %reshape.13.partner_ref, s32[504]{0:T(512)} %reshape.14.top_partner_ref, f32[3,32768]{1,0:T(4,128)} %pts_ref.1, f32[8,32768]{1,0:T(8,128)} %chg_ref.1, bf16[8192,128]{1,0:T(8,128)(2,1)} %bitcast.1, bf16[510,1024]{1,0:T(8,128)(2,1)} %transfer_hbm.1, ...), custom_call_target="tpu_custom_call" | custom-call | flops 40000000000 | bytes 16777216 | tf_op jit(solution)/shard_map/product/pallas_call | solution.py:580
  99.0 2.3 %copy.16 = f32[8,32768]{1,0:T(8,128)} copy(f32[8,32768]{1,0:T(8,128)} %product.1) | data formatting | bytes 2097152
  (1 shorter events, 0.0 us)
where the time goes:
time: 102 us; the launch traced here: 101 us
  Pallas kernels  94.3 us (92%)
  local copies, waits for them, and re-layouts  5.48 us (5%)
  other arithmetic  1.42 us (1%)
    pallas_call x1, Pallas kernels, on_device(): make_product(leaves, branches, near_list.shape[1], low_partner.shape[1],...  94.3 us
    unnamed x3, local copies, waits for them, and re-layouts  3.18 us

commit v1 on v0

--- a/solution.py
+++ b/solution.py
@@ -156,7 +156,8 @@
     span = leaves + 2 * reach
     edge = reach * 128
     length = leaves * 128
-    unroll = 4
+    unroll = 8
+    chunk = 4 * unroll
     wide = near_slots * 128
     top_rows = 2 * branches - 4
     rounds = rounds_of(branches)
@@ -167,14 +168,16 @@
         index_ref,
         partner_ref,
         top_partner_ref,
-        pts_ref,
-        chg_ref,
+        pts_hbm,
+        chg_hbm,
         basis_hbm,
         transfer_hbm,
         coupling_hbm,
         top_transfer_hbm,
         top_coupling_hbm,
         out_ref,
+        pts_ref,
+        chg_ref,
         basis_ref,
         transfer_ref,
         coupling_ref,
@@ -211,9 +214,11 @@
             pltpu.make_async_copy(a, b, load_sem.at[i])
             for i, (a, b) in enumerate(
                 (
+                    (chg_hbm, chg_ref),
                     (basis_hbm, basis_ref),
                     (transfer_hbm, transfer_ref),
                     (coupling_hbm, coupling_ref.at[0:rows]),
+                    (pts_hbm, pts_ref),
                     (top_transfer_hbm, top_transfer_ref),
                     (top_coupling_hbm, top_coupling_ref),
                 )
@@ -246,10 +251,10 @@
             )
 
         halos = [
-            remote(0, pts_ref.at[:, length - edge : length], pts_before_ref, right),
-            remote(1, chg_ref.at[:, length - edge : length], chg_before_ref, right),
-            remote(2, pts_ref.at[:, 0:edge], pts_after_ref, left),
-            remote(3, chg_ref.at[:, 0:edge], chg_after_ref, left),
+            remote(0, pts_hbm.at[:, length - edge : length], pts_before_ref, right),
+            remote(1, chg_hbm.at[:, length - edge : length], chg_before_ref, right),
+            remote(2, pts_hbm.at[:, 0:edge], pts_after_ref, left),
+            remote(3, chg_hbm.at[:, 0:edge], chg_after_ref, left),
         ]
         coef_halos = [
             remote(4, last_ref, before_ref, right),
@@ -269,7 +274,12 @@
         xmat_ref[...] = expand_matrix()
         rmat_ref[...] = reduce_matrix()
 
+        pl.semaphore_wait(barrier, 2 + len(peers))
+        for copy in halos:
+            copy.start()
+
         fetches[0].wait()
+        fetches[1].wait()
 
         def leaf_up(i, carry):
             at = pl.multiple_of(i * 1024, 1024)
@@ -287,11 +297,7 @@
 
         lax.fori_loop(0, leaves // 8, leaf_up, 0, unroll=4)
 
-        pl.semaphore_wait(barrier, 2 + len(peers))
-        for copy in halos:
-            copy.start()
-
-        fetches[1].wait()
+        fetches[2].wait()
         upcast_rows(e_ref, transfer_ref, rows - 1)
         for k in range(depth):
             start = level_start(leaves, k)
@@ -341,6 +347,7 @@
 
             lax.fori_loop(0, count // 8, step, 0)
 
+        fetches[4].wait()
         prepare(pts_ref, chg_ref, reach, True, leaves)
         for copy in halos:
             copy.wait_recv()
@@ -352,7 +359,8 @@
         def tiles_of(leaf, slot, j):
             target = tgt_ref[leaf]
             for s in range(near_slots):
-                q = index_ref[leaf * near_slots + s]
+                entry = index_ref[s, leaf]
+                q = jnp.where(entry >= 0, jnp.maximum(entry - me * leaves + reach, 0), span)
                 square = lax.dot_general(
                     src_ref[q], target, (((0,), (0,)), ((), ())), preferred_element_type=F32
                 )
@@ -364,29 +372,6 @@
             out_ref[:, pl.ds(at, 128)] = jnp.dot(
                 rhs_ref[slot, j].astype(BF16), tile_ref[slot, j], preferred_element_type=F32
             )
-
-        for j in range(unroll):
-            tiles_of(j, 0, j)
-
-        def near_step(i, carry):
-            for half in range(2):
-                base = (2 * i + half) * unroll
-                for j in range(unroll):
-                    tiles_of((base + unroll + j) % leaves, 1 - half, j)
-                for j in range(unroll):
-                    apply(base + j, half, j)
-            for r in range(1, len(rounds)):
-
-                @pl.when(i == (r * loop_steps) // (len(rounds) + 1))
-                def _():
-                    for copy in gathers[r - 1]:
-                        copy.wait_recv()
-                    for copy in gathers[r]:
-                        copy.start()
-
-            return carry
-
-        lax.fori_loop(0, loop_steps, near_step, 0)
 
         table_ref[3 * rows] = jnp.zeros((8, 128), F32)
         for copy in coef_halos:
@@ -404,29 +389,55 @@
                 at += counts[k]
 
         coupling_ref[rows] = jnp.zeros((slots, 1024), BF16)
-        fetches[2].wait()
-
-        def couple(i, carry):
-            first = i * 16
-            c_ref[...] = coupling_ref[pl.ds(first, 16)].reshape(16 * slots, 1024).astype(F32)
-            for n in range(16):
-                acc = [None] * 8
-                for s in range(slots):
-                    u = table_ref[partner_ref[(first + n) * slots + s]]
-                    row = spread_row(c_ref, n * slots + s)
-                    for j in range(8):
-                        piece = u * row[:, 128 * j : 128 * j + 128]
-                        acc[j] = piece if acc[j] is None else acc[j] + piece
+        fetches[3].wait()
+
+        def couple(first, n):
+            node = first + n
+            if n == chunk - 1:
+                node = node % rows
+            acc = [None] * 8
+            for s in range(slots):
+                entry = partner_ref[s, node]
+                at = jnp.maximum(entry - (me - 1) * rows, 0)
+                u = table_ref[jnp.where(entry >= 0, at, 3 * rows)]
+                row = spread_row(c_ref, n * slots + s)
                 for j in range(8):
-                    acc_ref[8 * n : 8 * n + 8, 128 * j : 128 * j + 128] = acc[j]
-            far = reduce32(acc_ref[0:128], rmat_ref[...])
-            far_ref[pl.ds(first, 16)] = far.reshape(16, 8, 128)
+                    piece = u * row[:, 128 * j : 128 * j + 128]
+                    acc[j] = piece if acc[j] is None else acc[j] + piece
+            for j in range(8):
+                acc_ref[8 * n : 8 * n + 8, 128 * j : 128 * j + 128] = acc[j]
+
+        for j in range(unroll):
+            tiles_of(j, 0, j)
+
+        def near_step(i, carry):
+            first = i * chunk
+            c_ref[...] = coupling_ref[pl.ds(first, chunk)].reshape(chunk * slots, 1024).astype(F32)
+            for half in range(2):
+                base = (2 * i + half) * unroll
+                for j in range(unroll):
+                    tiles_of((base + unroll + j) % leaves, 1 - half, j)
+                    for n in range(2):
+                        couple(first, 2 * (half * unroll + j) + n)
+                for j in range(unroll):
+                    apply(base + j, half, j)
+            far = jnp.dot(acc_ref[...].astype(BF16), rmat_ref[...], preferred_element_type=F32)
+            far_ref[pl.ds(first, chunk)] = far.reshape(chunk, 8, 128)
+            for r in range(1, len(rounds)):
+
+                @pl.when(i == (r * loop_steps) // (len(rounds) + 1))
+                def _():
+                    for copy in gathers[r - 1]:
+                        copy.wait_recv()
+                    for copy in gathers[r]:
+                        copy.start()
+
             return carry
 
-        lax.fori_loop(0, 2 * leaves // 16, couple, 0)
-
-        fetches[3].wait()
-        fetches[4].wait()
+        lax.fori_loop(0, loop_steps, near_step, 0)
+
+        fetches[5].wait()
+        fetches[6].wait()
         upcast_rows(top_e_ref, top_transfer_ref, top_rows)
         for copy in gathers[-1]:
             copy.wait_recv()
@@ -441,7 +452,7 @@
             mats = top_coupling_ref[row_at].astype(F32)
             acc = [None] * 8
             for s in range(top_slots):
-                entry = top_partner_ref[row_at * top_slots + s]
+                entry = top_partner_ref[s, row_at]
                 at = jnp.where(entry >= 0, level_start(branches, u) + entry, 2 * branches - 2)
                 value = upper_ref[at]
                 for j in range(8):
@@ -511,9 +522,11 @@
     return pl.pallas_call(
         kernel,
         out_shape=jax.ShapeDtypeStruct((8, length), F32),
-        in_specs=[smem] * 3 + [vmem] * 2 + [hbm] * 5,
+        in_specs=[smem] * 3 + [hbm] * 7,
         out_specs=vmem,
         scratch_shapes=[
+            pltpu.VMEM((3, length), F32),
+            pltpu.VMEM((8, length), F32),
             pltpu.VMEM((leaves * 32, 128), BF16),
             pltpu.VMEM((rows - 1, 1024), BF16),
             pltpu.VMEM((rows + 1, slots, 1024), BF16),
@@ -537,11 +550,11 @@
             pltpu.VMEM((span + 1, 8, 128), F32),
             pltpu.VMEM((2, unroll, wide, 128), BF16),
             pltpu.VMEM((2, unroll, 8, wide), F32),
-            pltpu.VMEM((16 * slots, 1024), F32),
-            pltpu.VMEM((8 * GROUP, 1024), F32),
+            pltpu.VMEM((chunk * slots, 1024), F32),
+            pltpu.VMEM((8 * chunk, 1024), F32),
             pltpu.VMEM((128, 1024), BF16),
             pltpu.VMEM((1024, 128), BF16),
-            pltpu.SemaphoreType.DMA((5,)),
+            pltpu.SemaphoreType.DMA((7,)),
             pltpu.SemaphoreType.DMA((n_copies,)),
             pltpu.SemaphoreType.DMA((n_copies,)),
         ],
@@ -570,19 +583,13 @@
     near_list,
 ):
     branches = lax.axis_size("branch")
-    me = lax.axis_index("branch")
     leaves = leaf_basis.shape[0]
-    rows = 2 * leaves - 1
-    reach = leaves // 4
-    near_rows = jnp.where(near_list >= 0, near_list - (me * leaves - reach), leaves + 2 * reach)
-    partner_rows = jnp.where(low_partner >= 0, low_partner - (me - 1) * rows, 3 * rows)
-    partner_rows = jnp.pad(partner_rows, ((0, 1), (0, 0)), constant_values=3 * rows)
     return make_product(
         leaves, branches, near_list.shape[1], low_partner.shape[1], top_partner.shape[1]
     )(
-        near_rows.reshape(-1),
-        partner_rows.reshape(-1),
-        top_partner.reshape(-1),
+        near_list.T,
+        low_partner.T,
+        top_partner.T,
         points,
         charges,
         leaf_basis.reshape(leaves * 32, 128),

time: 102 us -> 96.1 us (0.942)
  local copies, waits for them, and re-layouts: 5.48 us -> 2.26 us
  other arithmetic: 1.42 us -> 0 us
    reshape x3 -> x0, local copies, waits for them, and re-layouts: 2.16 us -> none  [the longest x1 0.75 us: on_device(): partner_rows.reshape(-1)]
    select_n x2 -> x0, other arithmetic: 1.42 us -> none  [the longest x1 0.72 us: on_device(): jnp.where(low_partner >= 0, low_partner - (me - 1) * rows, 3 * rows)]
    unnamed x3 -> x1, local copies, waits for them, and re-layouts: 3.18 us -> 2.26 us
where the time goes in v1:
time: 96.1 us; the launch traced here: 95.9 us
  Pallas kernels  93.6 us (97%)
  local copies, waits for them, and re-layouts  2.26 us (2%)
    pallas_call x1, Pallas kernels, on_device(): make_product(leaves, branches, near_list.shape[1], low_partner.shape[1],...  93.6 us
    unnamed x1, local copies, waits for them, and re-layouts  2.26 us

profile of v1, /device:TPU:0, one launch (start us, length us, event | category | flops | bytes accessed | tf_op | source)
XLA Modules:
  0.0 95.9 jit_solution(12588547294268276358)
XLA Ops:
  0.0 93.6 %product.1 = f32[8,32768]{1,0:T(8,128)} custom-call(s32[8,256]{1,0:T(8,128)} %bitcast.6, s32[8,511]{1,0:T(8,128)} %bitcast.5, s32[4,126]{1,0:T(4,128)} %bitcast.7, f32[3,32768]{1,0:T(4,128)} %pts_hbm.1, f32[8,32768]{1,0:T(8,128)} %chg_hbm.1, bf16[8192,128]{1,0:T(8,128)(2,1)} %bitcast.4, bf16[510,1024]{1,0:T(8,128)(2,1)} %transfer_hbm.1, ...), custom_call_target="tpu_custom_call" | custom-call | flops 40000000000 | bytes 16777216 | tf_op jit(solution)/shard_map/product/pallas_call | solution.py:587
  93.6 2.3 %copy.12 = f32[8,32768]{1,0:T(8,128)} copy(f32[8,32768]{1,0:T(8,128)} %product.1) | data formatting | bytes 2097152

commit v2 on v1

--- a/solution.py
+++ b/solution.py
@@ -12,7 +12,7 @@
 F32 = jnp.float32
 BF16 = jnp.bfloat16
 VMEM_BYTES = 60 << 20
-GROUP = 32
+GROUP = 128
 
 
 def level_start(total, depth_at):
@@ -163,10 +163,24 @@
     rounds = rounds_of(branches)
     n_round = sum(size - 1 for size, _ in rounds)
     loop_steps = leaves // (2 * unroll)
+    held = [1]
+    for r in range(1, len(rounds)):
+        held.append(4 * held[-1] + sum(min(2, 3 - n) for n in (1, 2) if 2 * r + n - 1 < depth_top))
+
+    def upper_row(level, node):
+        r = level // 2
+        bits = 1 if level % 2 == 0 else 0
+        row = (4 * held[r - 1] if r else 0) + (node & 1 if bits else (2 if r else 0))
+        block = node >> bits
+        for i in range(r + 1, len(rounds)):
+            row = row + (block & 3) * held[i - 1]
+            block = block >> 2
+        return row
+
 
     def kernel(
-        index_ref,
-        partner_ref,
+        near_list_ref,
+        low_partner_ref,
         top_partner_ref,
         pts_hbm,
         chg_hbm,
@@ -176,6 +190,10 @@
         top_transfer_hbm,
         top_coupling_hbm,
         out_ref,
+        near_rows_ref,
+        partner_rows_ref,
+        index_ref,
+        partner_ref,
         pts_ref,
         chg_ref,
         basis_ref,
@@ -193,6 +211,7 @@
         after_ref,
         table_ref,
         upper_ref,
+        roots_ref,
         far_ref,
         e_ref,
         top_e_ref,
@@ -260,16 +279,67 @@
             remote(4, last_ref, before_ref, right),
             remote(5, first_ref, after_ref, left),
         ]
+        digits = [(me // stride) % size for size, stride in rounds]
         gathers, at = [], 0
-        for size, stride in rounds:
-            block = pl.ds((me // stride) * stride, stride)
+        for r, (size, stride) in enumerate(rounds):
+            if r == 0:
+                block = roots_ref.at[pl.ds(digits[0], 1)]
+            else:
+                first = sum(digits[i] * held[i - 1] for i in range(r, len(rounds)))
+                block = upper_ref.at[pl.ds(first, held[r - 1])]
             gathers.append(
-                [
-                    remote(6 + at + t, upper_ref.at[block], upper_ref.at[block], peers[at + t])
-                    for t in range(size - 1)
-                ]
+                [remote(6 + at + t, block, block, peers[at + t]) for t in range(size - 1)]
             )
             at += size - 1
+
+        def lift(children, e_row):
+            wide = expand(jnp.concatenate(children, axis=0), xmat_ref[...])
+            parents = []
+            for n in range(0, len(children), 2):
+                total = None
+                for m in (n, n + 1):
+                    prod = wide[8 * m : 8 * m + 8] * top_e_ref[pl.ds(e_row + m, 1), :]
+                    for j in range(8):
+                        piece = prod[:, 128 * j : 128 * j + 128]
+                        total = piece if total is None else total + piece
+                parents.append(spread_groups(total))
+            return parents
+
+        def after_round(r):
+            for copy in gathers[r]:
+                copy.wait_recv()
+            if r == 0:
+                first = sum(digits[i] * held[i - 1] for i in range(1, len(rounds)))
+                upper_ref[first] = lift([roots_ref[0], roots_ref[1]], (me // 2) * 2)[0]
+                return
+            size, stride = rounds[r]
+            first = sum(digits[i] * held[i - 1] for i in range(r + 1, len(rounds)))
+            block = me // (size * stride)
+            level = 2 * r
+            children = [upper_ref[first + n * held[r - 1] + held[r - 1] - 1] for n in range(4)]
+            two = lift(children, level_start(branches, level - 1) + 4 * block)
+            for n in range(2):
+                upper_ref[first + 4 * held[r - 1] + n] = two[n]
+            if level + 1 < depth_top:
+                one = lift(two, level_start(branches, level) + 2 * block)
+                upper_ref[first + 4 * held[r - 1] + 2] = one[0]
+
+
+        entry = near_list_ref[...]
+        near_rows_ref[...] = jnp.where(
+            entry >= 0, jnp.maximum(entry - me * leaves + reach, 0), span
+        )
+        entry = low_partner_ref[...]
+        partner_rows_ref[...] = jnp.full((slots, rows + 1), 3 * rows, jnp.int32)
+        partner_rows_ref[:, 0:rows] = jnp.where(
+            entry >= 0, jnp.maximum(entry - (me - 1) * rows, 0), 3 * rows
+        )
+        lists = [
+            pltpu.make_async_copy(near_rows_ref, index_ref, load_sem.at[7]),
+            pltpu.make_async_copy(partner_rows_ref, partner_ref, load_sem.at[8]),
+        ]
+        for copy in lists:
+            copy.start()
 
         xmat_ref[...] = expand_matrix()
         rmat_ref[...] = reduce_matrix()
@@ -326,7 +396,7 @@
                 pack_ref[at // 4] = packed
         for copy in coef_halos:
             copy.start()
-        upper_ref[pl.ds(me, 1)] = table_ref[own + rows - 1 : own + rows]
+        roots_ref[pl.ds(digits[0], 1)] = table_ref[own + rows - 1 : own + rows]
         for copy in gathers[0]:
             copy.start()
 
@@ -359,8 +429,7 @@
         def tiles_of(leaf, slot, j):
             target = tgt_ref[leaf]
             for s in range(near_slots):
-                entry = index_ref[s, leaf]
-                q = jnp.where(entry >= 0, jnp.maximum(entry - me * leaves + reach, 0), span)
+                q = index_ref[s, leaf]
                 square = lax.dot_general(
                     src_ref[q], target, (((0,), (0,)), ((), ())), preferred_element_type=F32
                 )
@@ -393,13 +462,9 @@
 
         def couple(first, n):
             node = first + n
-            if n == chunk - 1:
-                node = node % rows
             acc = [None] * 8
             for s in range(slots):
-                entry = partner_ref[s, node]
-                at = jnp.maximum(entry - (me - 1) * rows, 0)
-                u = table_ref[jnp.where(entry >= 0, at, 3 * rows)]
+                u = table_ref[partner_ref[s, node]]
                 row = spread_row(c_ref, n * slots + s)
                 for j in range(8):
                     piece = u * row[:, 128 * j : 128 * j + 128]
@@ -407,6 +472,11 @@
             for j in range(8):
                 acc_ref[8 * n : 8 * n + 8, 128 * j : 128 * j + 128] = acc[j]
 
+        fetches[5].wait()
+        fetches[6].wait()
+        upcast_rows(top_e_ref, top_transfer_ref, top_rows)
+        for copy in lists:
+            copy.wait()
         for j in range(unroll):
             tiles_of(j, 0, j)
 
@@ -421,14 +491,13 @@
                         couple(first, 2 * (half * unroll + j) + n)
                 for j in range(unroll):
                     apply(base + j, half, j)
-            far = jnp.dot(acc_ref[...].astype(BF16), rmat_ref[...], preferred_element_type=F32)
+            far = jnp.dot(acc_ref[0 : 8 * chunk].astype(BF16), rmat_ref[...], preferred_element_type=F32)
             far_ref[pl.ds(first, chunk)] = far.reshape(chunk, 8, 128)
             for r in range(1, len(rounds)):
 
                 @pl.when(i == (r * loop_steps) // (len(rounds) + 1))
                 def _():
-                    for copy in gathers[r - 1]:
-                        copy.wait_recv()
+                    after_round(r - 1)
                     for copy in gathers[r]:
                         copy.start()
 
@@ -436,24 +505,15 @@
 
         lax.fori_loop(0, loop_steps, near_step, 0)
 
-        fetches[5].wait()
-        fetches[6].wait()
-        upcast_rows(top_e_ref, top_transfer_ref, top_rows)
-        for copy in gathers[-1]:
-            copy.wait_recv()
-        for u in range(depth_top - 1):
-            src = level_start(branches, u)
-            move_up(
-                upper_ref, top_e_ref, xmat_ref, src, level_start(branches, u + 1), src, branches >> u
-            )
-        upper_ref[2 * branches - 2] = jnp.zeros((8, 128), F32)
+        after_round(len(rounds) - 1)
+        upper_ref[held[-1]] = jnp.zeros((8, 128), F32)
         for u in range(1, depth_top):
             row_at = level_start(branches, u) - branches + me // (1 << u)
             mats = top_coupling_ref[row_at].astype(F32)
             acc = [None] * 8
             for s in range(top_slots):
                 entry = top_partner_ref[s, row_at]
-                at = jnp.where(entry >= 0, level_start(branches, u) + entry, 2 * branches - 2)
+                at = jnp.where(entry >= 0, upper_row(u, jnp.maximum(entry, 0)), held[-1])
                 value = upper_ref[at]
                 for j in range(8):
                     piece = value * mats[s : s + 1, 128 * j : 128 * j + 128]
@@ -522,9 +582,13 @@
     return pl.pallas_call(
         kernel,
         out_shape=jax.ShapeDtypeStruct((8, length), F32),
-        in_specs=[smem] * 3 + [hbm] * 7,
+        in_specs=[vmem] * 2 + [smem] + [hbm] * 7,
         out_specs=vmem,
         scratch_shapes=[
+            pltpu.VMEM((near_slots, leaves), jnp.int32),
+            pltpu.VMEM((slots, rows + 1), jnp.int32),
+            pltpu.SMEM((near_slots, leaves), jnp.int32),
+            pltpu.SMEM((slots, rows + 1), jnp.int32),
             pltpu.VMEM((3, length), F32),
             pltpu.VMEM((8, length), F32),
             pltpu.VMEM((leaves * 32, 128), BF16),
@@ -541,7 +605,8 @@
             pltpu.VMEM((packs, 8, 128), F32),
             pltpu.VMEM((packs, 8, 128), F32),
             pltpu.VMEM((3 * rows + 1, 8, 128), F32),
-            pltpu.VMEM((2 * branches - 1, 8, 128), F32),
+            pltpu.VMEM((held[-1] + 1, 8, 128), F32),
+            pltpu.VMEM((2, 8, 128), F32),
             pltpu.VMEM((rows + 1, 8, 128), F32),
             pltpu.VMEM((rows - 1, 1024), F32),
             pltpu.VMEM((top_rows, 1024), F32),
@@ -551,10 +616,10 @@
             pltpu.VMEM((2, unroll, wide, 128), BF16),
             pltpu.VMEM((2, unroll, 8, wide), F32),
             pltpu.VMEM((chunk * slots, 1024), F32),
-            pltpu.VMEM((8 * chunk, 1024), F32),
+            pltpu.VMEM((8 * max(chunk, GROUP), 1024), F32),
             pltpu.VMEM((128, 1024), BF16),
             pltpu.VMEM((1024, 128), BF16),
-            pltpu.SemaphoreType.DMA((7,)),
+            pltpu.SemaphoreType.DMA((9,)),
             pltpu.SemaphoreType.DMA((n_copies,)),
             pltpu.SemaphoreType.DMA((n_copies,)),
         ],

time: 96.1 us -> 84.7 us (0.88)
  Pallas kernels: 93.6 us -> 82.3 us
    pallas_call x1, Pallas kernels: 93.6 us -> 82.3 us  [on_device(): make_product(leaves, branches, near_list.shape[1], low_partner.shape[1],...]
where the time goes in v2:
time: 84.7 us; the launch traced here: 84.5 us
  Pallas kernels  82.3 us (97%)
  local copies, waits for them, and re-layouts  2.26 us (3%)
    pallas_call x1, Pallas kernels, on_device(): make_product(leaves, branches, near_list.shape[1], low_partner.shape[1],...  82.3 us
    unnamed x1, local copies, waits for them, and re-layouts  2.26 us

profile of v2, /device:TPU:0, one launch (start us, length us, event | category | flops | bytes accessed | tf_op | source)
XLA Modules:
  0.0 84.5 jit_solution(323382262169666338)
XLA Ops:
  0.0 82.3 %product.1 = f32[8,32768]{1,0:T(8,128)} custom-call(s32[8,256]{1,0:T(8,128)} %bitcast.6, s32[8,511]{1,0:T(8,128)} %bitcast.5, s32[4,126]{1,0:T(4,128)} %bitcast.7, f32[3,32768]{1,0:T(4,128)} %pts_hbm.1, f32[8,32768]{1,0:T(8,128)} %chg_hbm.1, bf16[8192,128]{1,0:T(8,128)(2,1)} %bitcast.4, bf16[510,1024]{1,0:T(8,128)(2,1)} %transfer_hbm.1, ...), custom_call_target="tpu_custom_call" | custom-call | flops 40000000000 | bytes 16777216 | tf_op jit(solution)/shard_map/product/pallas_call | solution.py:652
  82.3 2.3 %copy.12 = f32[8,32768]{1,0:T(8,128)} copy(f32[8,32768]{1,0:T(8,128)} %product.1) | data formatting | bytes 2097152

commit v3 on v2

--- a/solution.py
+++ b/solution.py
@@ -344,10 +344,6 @@
         xmat_ref[...] = expand_matrix()
         rmat_ref[...] = reduce_matrix()
 
-        pl.semaphore_wait(barrier, 2 + len(peers))
-        for copy in halos:
-            copy.start()
-
         fetches[0].wait()
         fetches[1].wait()
 
@@ -365,10 +361,14 @@
                 table_ref[own + i * 8 + g] = spread_groups(jnp.where(group == g % 4, piece, 0.0))
             return carry
 
-        lax.fori_loop(0, leaves // 8, leaf_up, 0, unroll=4)
+        lax.fori_loop(0, leaves // 8, leaf_up, 0, unroll=8)
 
         fetches[2].wait()
         upcast_rows(e_ref, transfer_ref, rows - 1)
+        pl.semaphore_wait(barrier, 2 + len(peers))
+        for copy in halos:
+            copy.start()
+
         for k in range(depth):
             start = level_start(leaves, k)
             move_up(
@@ -415,7 +415,7 @@
                         tgt_ref[i * 8 + g] = target[:, 128 * g : 128 * g + 128]
                 return carry
 
-            lax.fori_loop(0, count // 8, step, 0)
+            lax.fori_loop(0, count // 8, step, 0, unroll=4)
 
         fetches[4].wait()
         prepare(pts_ref, chg_ref, reach, True, leaves)
@@ -571,7 +571,7 @@
                 out_ref[:, at] = out_ref[:, at] + values[8 * g : 8 * g + 8]
             return carry
 
-        lax.fori_loop(0, leaves // 8, leaf_down, 0, unroll=4)
+        lax.fori_loop(0, leaves // 8, leaf_down, 0, unroll=8)
         for copy in halos + coef_halos + [copy for group in gathers for copy in group]:
             copy.wait_send()
 

time: 84.7 us -> 83.7 us (0.988)
  Pallas kernels: 82.3 us -> 81.2 us
    pallas_call x1, Pallas kernels: 82.3 us -> 81.2 us  [on_device(): make_product(leaves, branches, near_list.shape[1], low_partner.shape[1],...]
where the time goes in v3:
time: 83.7 us; the launch traced here: 83.5 us
  Pallas kernels  81.2 us (97%)
  local copies, waits for them, and re-layouts  2.26 us (3%)
    pallas_call x1, Pallas kernels, on_device(): make_product(leaves, branches, near_list.shape[1], low_partner.shape[1],...  81.2 us
    unnamed x1, local copies, waits for them, and re-layouts  2.26 us

profile of v3, /device:TPU:0, one launch (start us, length us, event | category | flops | bytes accessed | tf_op | source)
XLA Modules:
  0.0 83.5 jit_solution(11887628370623792751)
XLA Ops:
  0.0 81.2 %product.1 = f32[8,32768]{1,0:T(8,128)} custom-call(s32[8,256]{1,0:T(8,128)} %bitcast.6, s32[8,511]{1,0:T(8,128)} %bitcast.5, s32[4,126]{1,0:T(4,128)} %bitcast.7, f32[3,32768]{1,0:T(4,128)} %pts_hbm.1, f32[8,32768]{1,0:T(8,128)} %chg_hbm.1, bf16[8192,128]{1,0:T(8,128)(2,1)} %bitcast.4, bf16[510,1024]{1,0:T(8,128)(2,1)} %transfer_hbm.1, ...), custom_call_target="tpu_custom_call" | custom-call | flops 40000000000 | bytes 16777216 | tf_op jit(solution)/shard_map/product/pallas_call | solution.py:652
  81.3 2.3 %copy.12 = f32[8,32768]{1,0:T(8,128)} copy(f32[8,32768]{1,0:T(8,128)} %product.1) | data formatting | bytes 2097152

commit v4 on v3

--- a/solution.py
+++ b/solution.py
@@ -157,12 +157,14 @@
     edge = reach * 128
     length = leaves * 128
     unroll = 8
-    chunk = 4 * unroll
+    chunk = 8 * unroll
     wide = near_slots * 128
     top_rows = 2 * branches - 4
     rounds = rounds_of(branches)
     n_round = sum(size - 1 for size, _ in rounds)
-    loop_steps = leaves // (2 * unroll)
+    inner = leaves - 2 * reach
+    loop_steps = inner // (2 * unroll)
+    starts = ((0, 5), (1, 1), (1, 4))
     held = [1]
     for r in range(1, len(rounds)):
         held.append(4 * held[-1] + sum(min(2, 3 - n) for n in (1, 2) if 2 * r + n - 1 < depth_top))
@@ -216,6 +218,8 @@
         e_ref,
         top_e_ref,
         src_ref,
+        own_src_ref,
+        own_load_ref,
         tgt_ref,
         load_ref,
         tile_ref,
@@ -326,9 +330,13 @@
 
 
         entry = near_list_ref[...]
-        near_rows_ref[...] = jnp.where(
-            entry >= 0, jnp.maximum(entry - me * leaves + reach, 0), span
+        leaf = lax.broadcasted_iota(jnp.int32, entry.shape, 1)
+        alone = (leaf >= reach) & (leaf < leaves - reach)
+        at = entry - me * leaves
+        at = jnp.where(
+            alone, jnp.clip(at, 0, leaves - 1), jnp.clip(at + reach, 0, span - 1)
         )
+        near_rows_ref[...] = jnp.where(entry >= 0, at, jnp.where(alone, leaves, span))
         entry = low_partner_ref[...]
         partner_rows_ref[...] = jnp.full((slots, rows + 1), 3 * rows, jnp.int32)
         partner_rows_ref[:, 0:rows] = jnp.where(
@@ -365,10 +373,6 @@
 
         fetches[2].wait()
         upcast_rows(e_ref, transfer_ref, rows - 1)
-        pl.semaphore_wait(barrier, 2 + len(peers))
-        for copy in halos:
-            copy.start()
-
         for k in range(depth):
             start = level_start(leaves, k)
             move_up(
@@ -394,7 +398,8 @@
                 for g in range(1, len(four)):
                     packed = jnp.where(lane == g, table_ref[own + four[g]], packed)
                 pack_ref[at // 4] = packed
-        for copy in coef_halos:
+        pl.semaphore_wait(barrier, 2 + len(peers))
+        for copy in halos + coef_halos:
             copy.start()
         roots_ref[pl.ds(digits[0], 1)] = table_ref[own + rows - 1 : own + rows]
         for copy in gathers[0]:
@@ -412,6 +417,8 @@
                 if is_own:
                     target = target_rows(*parts)
                     for g in range(8):
+                        own_src_ref[i * 8 + g] = source[:, 128 * g : 128 * g + 128]
+                        own_load_ref[i * 8 + g] = loads[:, 128 * g : 128 * g + 128]
                         tgt_ref[i * 8 + g] = target[:, 128 * g : 128 * g + 128]
                 return carry
 
@@ -419,28 +426,63 @@
 
         fetches[4].wait()
         prepare(pts_ref, chg_ref, reach, True, leaves)
+        own_src_ref[leaves] = own_src_ref[0]
+        own_load_ref[leaves] = jnp.zeros((8, 128), F32)
+
+        def tiles_of(leaf, slot, j, sources, charges):
+            target = tgt_ref[leaf]
+            for s in range(near_slots):
+                q = index_ref[s, leaf]
+                square = lax.dot_general(
+                    sources[q], target, (((0,), (0,)), ((), ())), preferred_element_type=F32
+                )
+                tile_ref[slot, j, 128 * s : 128 * s + 128, :] = lax.rsqrt(square).astype(BF16)
+                rhs_ref[slot, j, :, 128 * s : 128 * s + 128] = charges[q]
+
+        def apply(leaf, slot, j):
+            at = pl.multiple_of(leaf * 128, 128)
+            out_ref[:, pl.ds(at, 128)] = jnp.dot(
+                rhs_ref[slot, j].astype(BF16), tile_ref[slot, j], preferred_element_type=F32
+            )
+
+        fetches[5].wait()
+        fetches[6].wait()
+        upcast_rows(top_e_ref, top_transfer_ref, top_rows)
+        for copy in lists:
+            copy.wait()
+
+        def start_rounds(part, i):
+            for r in range(1, len(rounds)):
+                if starts[r - 1][0] == part:
+
+                    @pl.when(i == starts[r - 1][1])
+                    def _():
+                        after_round(r - 1)
+                        for copy in gathers[r]:
+                            copy.start()
+
+        for j in range(unroll):
+            tiles_of(reach + j, 0, j, own_src_ref, own_load_ref)
+
+        def inner_step(i, carry):
+            for half in range(2):
+                base = (2 * i + half) * unroll
+                for j in range(unroll):
+                    leaf = reach + (base + unroll + j) % inner
+                    tiles_of(leaf, 1 - half, j, own_src_ref, own_load_ref)
+                for j in range(unroll):
+                    apply(reach + base + j, half, j)
+            start_rounds(0, i)
+            return carry
+
+        lax.fori_loop(0, loop_steps, inner_step, 0)
+
         for copy in halos:
             copy.wait_recv()
         prepare(pts_before_ref, chg_before_ref, 0, False, reach)
         prepare(pts_after_ref, chg_after_ref, reach + leaves, False, reach)
         src_ref[span] = src_ref[reach]
         load_ref[span] = jnp.zeros((8, 128), F32)
-
-        def tiles_of(leaf, slot, j):
-            target = tgt_ref[leaf]
-            for s in range(near_slots):
-                q = index_ref[s, leaf]
-                square = lax.dot_general(
-                    src_ref[q], target, (((0,), (0,)), ((), ())), preferred_element_type=F32
-                )
-                tile_ref[slot, j, 128 * s : 128 * s + 128, :] = lax.rsqrt(square).astype(BF16)
-                rhs_ref[slot, j, :, 128 * s : 128 * s + 128] = load_ref[q]
-
-        def apply(leaf, slot, j):
-            at = pl.multiple_of(leaf * 128, 128)
-            out_ref[:, pl.ds(at, 128)] = jnp.dot(
-                rhs_ref[slot, j].astype(BF16), tile_ref[slot, j], preferred_element_type=F32
-            )
 
         table_ref[3 * rows] = jnp.zeros((8, 128), F32)
         for copy in coef_halos:
@@ -472,38 +514,28 @@
             for j in range(8):
                 acc_ref[8 * n : 8 * n + 8, 128 * j : 128 * j + 128] = acc[j]
 
-        fetches[5].wait()
-        fetches[6].wait()
-        upcast_rows(top_e_ref, top_transfer_ref, top_rows)
-        for copy in lists:
-            copy.wait()
         for j in range(unroll):
-            tiles_of(j, 0, j)
-
-        def near_step(i, carry):
+            tiles_of(leaves - reach + j, 0, j, src_ref, load_ref)
+
+        def outer_step(i, carry):
             first = i * chunk
             c_ref[...] = coupling_ref[pl.ds(first, chunk)].reshape(chunk * slots, 1024).astype(F32)
             for half in range(2):
-                base = (2 * i + half) * unroll
+                base = leaves - reach + (2 * i + half) * unroll
                 for j in range(unroll):
-                    tiles_of((base + unroll + j) % leaves, 1 - half, j)
-                    for n in range(2):
-                        couple(first, 2 * (half * unroll + j) + n)
+                    tiles_of((base + unroll + j) % leaves, 1 - half, j, src_ref, load_ref)
+                    for n in range(4):
+                        couple(first, 4 * (half * unroll + j) + n)
                 for j in range(unroll):
-                    apply(base + j, half, j)
-            far = jnp.dot(acc_ref[0 : 8 * chunk].astype(BF16), rmat_ref[...], preferred_element_type=F32)
+                    apply((base + j) % leaves, half, j)
+            far = jnp.dot(
+                acc_ref[0 : 8 * chunk].astype(BF16), rmat_ref[...], preferred_element_type=F32
+            )
             far_ref[pl.ds(first, chunk)] = far.reshape(chunk, 8, 128)
-            for r in range(1, len(rounds)):
-
-                @pl.when(i == (r * loop_steps) // (len(rounds) + 1))
-                def _():
-                    after_round(r - 1)
-                    for copy in gathers[r]:
-                        copy.start()
-
+            start_rounds(1, i)
             return carry
 
-        lax.fori_loop(0, loop_steps, near_step, 0)
+        lax.fori_loop(0, loop_steps, outer_step, 0)
 
         after_round(len(rounds) - 1)
         upper_ref[held[-1]] = jnp.zeros((8, 128), F32)
@@ -611,6 +643,8 @@
             pltpu.VMEM((rows - 1, 1024), F32),
             pltpu.VMEM((top_rows, 1024), F32),
             pltpu.VMEM((span + 1, 32, 128), BF16),
+            pltpu.VMEM((leaves + 1, 32, 128), BF16),
+            pltpu.VMEM((leaves + 1, 8, 128), F32),
             pltpu.VMEM((leaves, 32, 128), BF16),
             pltpu.VMEM((span + 1, 8, 128), F32),
             pltpu.VMEM((2, unroll, wide, 128), BF16),

time: 83.7 us -> 76.3 us (0.912)
  Pallas kernels: 81.2 us -> 73.7 us
    pallas_call x1, Pallas kernels: 81.2 us -> 73.7 us  [on_device(): make_product(leaves, branches, near_list.shape[1], low_partner.shape[1],...]
where the time goes in v4:
time: 76.3 us; the launch traced here: 76 us
  Pallas kernels  73.7 us (97%)
  local copies, waits for them, and re-layouts  2.26 us (3%)
    pallas_call x1, Pallas kernels, on_device(): make_product(leaves, branches, near_list.shape[1], low_partner.shape[1],...  73.7 us
    unnamed x1, local copies, waits for them, and re-layouts  2.26 us

profile of v4, /device:TPU:0, one launch (start us, length us, event | category | flops | bytes accessed | tf_op | source)
XLA Modules:
  0.0 76.0 jit_solution(13326717522503729356)
XLA Ops:
  0.0 73.7 %product.1 = f32[8,32768]{1,0:T(8,128)} custom-call(s32[8,256]{1,0:T(8,128)} %bitcast.6, s32[8,511]{1,0:T(8,128)} %bitcast.5, s32[4,126]{1,0:T(4,128)} %bitcast.7, f32[3,32768]{1,0:T(4,128)} %pts_hbm.1, f32[8,32768]{1,0:T(8,128)} %chg_hbm.1, bf16[8192,128]{1,0:T(8,128)(2,1)} %bitcast.4, bf16[510,1024]{1,0:T(8,128)(2,1)} %transfer_hbm.1, ...), custom_call_target="tpu_custom_call" | custom-call | flops 40000000000 | bytes 16777216 | tf_op jit(solution)/shard_map/product/pallas_call | solution.py:686
  73.7 2.3 %copy.12 = f32[8,32768]{1,0:T(8,128)} copy(f32[8,32768]{1,0:T(8,128)} %product.1) | data formatting | bytes 2097152
